TPU v7x, 256 devices: a whole 4x4x8 slice. The times are simulated.
256 devices in a mesh: chan: 64 (over y_hi, x, z), win: 4 (over y_lo, core).
Axes of the slice: x: 4, y: 4 (y_hi: 2, y_lo: 2; y = y_hi * 2 + y_lo), z: 8, core: 2. Of those that a mesh axis runs over, the one named last changes fastest.
Arguments:
- spectra: bfloat16 [64, 128, 128, 2, 128], P('chan', None, 'win'), may hold values from -6 to 6
- counts: int32 [128, 64], P('win'), may hold values from 1 to 256
- partner: int32 [2, 64], replicated, may hold values from 0 to 63, as said below
Outputs:
- cross: bfloat16 [64, 2, 128, 128, 256], P('win', None, 'chan')
Inputs may be any that keep to these rules, and one draw needn't show every extreme that they name: Each row of partner is one cycle through all 64 blocks: a permutation with no block its own partner and no two blocks each other's partners.
All inputs are finite; a program needn't handle non-finite values.
Results may differ from a plain program's by a relative error of at most 0.015.
Values may be sent and summed in bfloat16 or wider, within the bound.
No kernel may reach another device: no remote copies, remote signals or barrier semaphores. Data moves between devices by JAX's collectives and lax.ppermute only.
A program may use at most 128 MiB of HBM per device.

v0:
```python
import jax
import jax.numpy as jnp
from jax import lax
from jax.sharding import PartitionSpec as P

W_DEV = 32
NSAMP = 256
EPS = 1e-06


def stack_blocks(blocks, scale, mate_index, first, count):
    own = lax.dynamic_slice_in_dim(blocks, first, count, 0)
    mates = jnp.take(blocks, mate_index, axis=0)
    weighted = (scale[:, :, None, :, :, None, None] * own[:, None]).astype(jnp.bfloat16)
    rotated = jnp.stack([-mates[..., 1, :], mates[..., 0, :]], axis=-2)
    paired = jnp.stack([mates, rotated], axis=-2)
    return jnp.einsum(
        "nrfgwkc,nrfgwkod->nrfgcod", weighted, paired, preferred_element_type=jnp.float32
    )


def weights_of(tallies, partner):
    columns = tallies.astype(jnp.float32).T
    return jnp.minimum(columns[None], jnp.take(columns, partner, axis=0)) / NSAMP


def per_device(spectra, counts, partner):
    values = spectra.astype(jnp.float32)
    power = jnp.mean(jnp.sum(values * values, axis=3), axis=1)
    whitened = (values * lax.rsqrt(power + EPS)[:, None, :, None, :]).astype(jnp.bfloat16)
    mixed = lax.all_to_all(whitened, "chan", split_axis=1, concat_axis=0, tiled=True)
    nblocks = partner.shape[1]
    width = mixed.shape[4]
    local_bins = mixed.shape[1]
    rounds = partner.shape[0]
    groups = lax.axis_size("win")
    chosen = nblocks // groups
    first = lax.axis_index("win") * chosen
    gathered = lax.all_gather(mixed, "win", axis=2, tiled=True)
    tallies = lax.all_gather(counts, "win", axis=0, tiled=True)
    weight = weights_of(tallies, partner)
    norm = jnp.sqrt(jnp.sum(weight * weight, axis=2))
    blocks = gathered.reshape(nblocks, local_bins, groups, W_DEV, 2, width)
    own_scales = jnp.transpose(lax.dynamic_slice_in_dim(weight, first, chosen, 1), (1, 0, 2))
    scale = own_scales.reshape(chosen, rounds, groups, W_DEV)
    mate_index = jnp.transpose(lax.dynamic_slice_in_dim(partner, first, chosen, 1))
    partial_value = stack_blocks(blocks, scale, mate_index, first, chosen)
    partial_value = lax.optimization_barrier(partial_value.astype(jnp.bfloat16))
    total = jnp.sum(partial_value.astype(jnp.float32), axis=3)
    norm_rows = jnp.transpose(lax.dynamic_slice_in_dim(norm, first, chosen, 1))
    shaped = total.reshape(chosen, rounds, local_bins, width, 2 * width)
    result = shaped / norm_rows[:, :, None, None, None]
    return result.astype(jnp.bfloat16)


def solution(mesh):
    placed = (P("chan", None, "win", None, None), P("win", None), P())
    return jax.shard_map(
        per_device,
        mesh=mesh,
        in_specs=placed,
        out_specs=P("win", None, "chan", None, None),
        check_vma=False,
    )
```

profile of v0, /device:TPU:1, one launch (start us, length us, event | category | flops | bytes accessed | tf_op | source)
XLA Modules:
  0.0 240.4 jit_solution(3108517690756288380)
XLA Ops:
  6.5 0.0 all-gather.2.cloned.1.call-start
  6.5 3.8 %fusion.4 = f32[32,128]{1,0:T(8,128)S(1)} fusion(bf16[1,128,32,2,128]{4,3,2,1,0:T(2,128)(2,1)} %param.3), kind=kLoop, calls=%fused_computation.12 | loop fusion | flops 3141632 | bytes 2113536 | tf_op jit(solution)/shard_map/reduce_sum | solution.py:29
  10.4 3.8 %fusion.5 = bf16[1,128,32,2,128]{4,3,2,0,1:T(2,128)(2,1)S(1)} fusion(bf16[1,128,32,2,128]{4,3,2,1,0:T(2,128)(2,1)} %param.3, f32[32,128]{1,0:T(8,128)S(1)} %add_rsqrt_fusion), kind=kLoop, calls=%fused_computation.13 | loop fusion | flops 3145728 | bytes 4210688 | tf_op jit(solution)/shard_map/convert_element_type | solution.py:30
  14.2 63.5 %all_to_all.12 = bf16[1,128,32,2,128]{4,3,2,0,1:T(2,128)(2,1)S(1)} all-to-all(bf16[1,128,32,2,128]{4,3,2,0,1:T(2,128)(2,1)S(1)} %fusion.5), channel_id=1, replica_groups=mesh['chan'=64,'win'=4] {'chan'}, dimensions={1} | all-to-all | bytes 4194304 | tf_op jit(solution)/shard_map/all_to_all | solution.py:31
  77.7 0.0 copy-start.2
  77.7 0.0 copy-start.1
  77.7 1.9 copy.36
  79.6 0.0 all-gather.2.cloned.1.call-update
  79.6 0.0 copy-done.2
  79.6 0.1 compare_and_fusion
  79.7 0.1 copy.39
  79.8 0.1 reshape.56
  79.9 0.1 copy.38
  80.0 0.0 copy-done.1
  80.0 9.0 %all_gather.6 = s32[128,64]{1,0:T(8,128)S(1)} all-gather(s32[32,64]{1,0:T(8,128)S(1)} %copy-done.1), channel_id=1, replica_groups=mesh['chan'=64,'win'=4] {'win'}, dimensions={0}, use_global_device_ids=true | all-gather | bytes 40960 | tf_op jit(solution)/shard_map/all_gather | solution.py:40
  89.0 0.1 copy.33
  89.1 0.1 reshape.48
  89.2 0.6 gather_fusion
  89.9 0.2 multiply_reduce_fusion
  90.1 0.1 mul.33
  90.2 0.1 dynamic-slice_bitcast_fusion.1
  90.3 0.1 copy.43
  90.3 72.9 %all-gather.2.cloned.1.call-done = bf16[64,2,128,2,128]{4,2,3,1,0:T(8,128)(2,1)} async-done(((bf16[64,2,32,2,128]{4,2,3,1,0:T(8,128)(2,1)}), bf16[64,2,128,2,128]{4,2,3,1,0:T(8,128)(2,1)}) %all-gather.2.cloned.1.call-update) | async-done | bytes 8388624 | tf_op jit(solution)/shard_map/all_gather | solution.py:39
  163.2 9.2 %copy.40 = bf16[64,2,4,32,2,128]{5,3,4,2,1,0:T(8,128)(2,1)} copy(bf16[64,2,4,32,2,128]{5,3,2,4,1,0:T(8,128)(2,1)} %bitcast.35) | data formatting | bytes 16777216 | tf_op jit(solution)/shard_map/reshape | solution.py:43
  172.4 6.5 %gather_fusion.1 = bf16[32,2,4,32,2,128]{5,3,4,2,1,0:T(8,128)(2,1)} fusion(bf16[64,2,4,32,2,128]{5,3,4,2,1,0:T(8,128)(2,1)} %copy.40, s32[1024]{0:T(1024)S(1)} %pad_clamp_fusion), kind=kCustom, calls=%fused_computation.1 | custom fusion | bytes 8388736 | tf_op jit(solution)/shard_map/jit(_take)/gather | solution.py:13
  178.8 2.6 %broadcast_select_fusion = bf16[16,2,2,4,32,2,128]{6,4,5,3,2,1,0:T(8,128)(2,1)S(1)} fusion(bf16[16,2,2,4,32,2,128]{6,4,5,3,2,1,0:T(8,128)(2,1)} %bitcast.33, pred[16,2]{1,0:T(8,128)(4,1)S(1)} %copy.38), kind=kLoop, calls=%fused_computation.18 | loop fusion | flops 2097152 | bytes 8388640 | tf_op jit(solution)/shard_map/jit(_take)/select_n | solution.py:13
  181.5 0.0 copy-start
  181.5 0.4 slice_negate_fusion
  181.9 1.8 copy-done
  183.7 0.5 broadcast_select_fusion.1
  184.2 2.4 maximum_bitcast_fusion
  186.5 11.9 %bitcast_convert_fusion = bf16[16,2,2,4,128,2,128]{6,4,5,3,2,1,0:T(8,128)(2,1)} fusion(bf16[16,2,2,4,32,2,1,128]{7,4,5,6,3,2,1,0:T(8,128)(2,1)} %maximum_bitcast_fusion, bf16[16,2,2,4,32,2,1,128]{7,4,5,6,3,2,1,0:T(8,128)(2,1)S(1)} %broadcast_select_fusion.1, f32[16,2,4,32]{3,2,0,1:T(4,128)S(1)} %mul.33, bf16[64,2,4,32,2,128]{5,3,2,4,1,0:T(8,128)(2,1)} %bitcast.36, ...), kind=kOutput, calls=%fused_computation.2 | convolution fusion | flops 1104150528 | bytes 27279364 | tf_op jit(solution)/shard_map/nrfgwkc,nrfgwkod->nrfgcod/dot_general | solution.py:17
  198.4 13.0 %convert_reduce_fusion = f32[16,2,2,128,2,128]{5,3,4,2,1,0:T(8,128)} fusion(bf16[16,2,2,4,128,2,128]{6,4,5,3,2,1,0:T(8,128)(2,1)} %bitcast_convert_fusion), kind=kLoop, calls=%fused_computation.3 | loop fusion | flops 14680064 | bytes 25165824 | tf_op jit(solution)/shard_map/reduce_sum | solution.py:49
  211.4 9.3 %copy.42 = f32[16,2,2,128,2,128]{3,5,4,2,1,0:T(8,128)} copy(f32[16,2,2,128,2,128]{5,3,4,2,1,0:T(8,128)} %convert_reduce_fusion) | data formatting | bytes 16777216 | tf_op jit(solution)/shard_map/reduce_sum | solution.py:49
  220.7 6.5 %fusion.3 = bf16[16,2,2,128,256]{3,4,2,1,0:T(8,128)(2,1)} fusion(f32[16,2,2,128,2,128]{3,5,4,2,1,0:T(8,128)} %copy.42, f32[16,2]{1,0:T(8,128)S(1)} %copy.43), kind=kLoop, calls=%fused_computation.8 | loop fusion | flops 4194304 | bytes 12583040 | tf_op jit(solution)/shard_map/convert_element_type | solution.py:53
  227.2 6.4 %copy.44 = bf16[16,2,2,128,256]{4,3,2,1,0:T(8,128)(2,1)} copy(bf16[16,2,2,128,256]{3,4,2,1,0:T(8,128)(2,1)} %fusion.3) | data formatting | bytes 8388608 | tf_op jit(solution)/shard_map/convert_element_type | solution.py:53
  (8 shorter events, 0.1 us)
Async XLA Ops:
  6.5 156.7 %all-gather.2.cloned.1.call-start = ((), (), s32[]{:S(2)}) async-start(), calls=%async_computation.1 | async-start | bytes 10485760 | tf_op jit(solution)/shard_map/all_gather | solution.py:39
  77.7 1.9 copy-start.2
  77.7 2.3 copy-start.1
  181.5 2.2 copy-start
Sparse Core Ops, SparseCore 0:
  79.7 83.4 all-gather.1
where the time goes:
time: 241 us; the launch traced here: 240 us
  waiting for transfers between devices  72.9 us (30%)
  blocking collectives  72.6 us (30%)
  local copies, waits for them, and re-layouts  36.3 us (15%)
  other arithmetic  33.3 us (14%)
  between operations  13.5 us (6%)
  matrix products  11.9 us (5%)
    all_gather x1, waiting for transfers between devices, per_device(): gathered = lax.all_gather(mixed, 'win', axis=2, tiled=True)  72.9 us
    all_to_all x1, blocking collectives, per_device(): lax.all_to_all(whitened, 'chan', split_axis=1, concat_axis=0, tiled=True)  63.5 us
    reduce_sum x1, other arithmetic, per_device(): total = jnp.sum(partial_value.astype(jnp.float32), axis=3)  13 us
    dot_general x1, matrix products, stack_blocks(): jnp.einsum('nrfgwkc,nrfgwkod->nrfgcod', weighted, paired, preferred_eleme...  11.9 us
    reduce_sum x1, local copies, waits for them, and re-layouts, per_device(): total = jnp.sum(partial_value.astype(jnp.float32), axis=3)  9.27 us
    reshape x1, local copies, waits for them, and re-layouts, per_device(): blocks = gathered.reshape(nblocks, local_bins, groups, W_DEV, 2, width)  9.15 us
    all_gather x1, blocking collectives, per_device(): tallies = lax.all_gather(counts, 'win', axis=0, tiled=True)  9.03 us
    convert_element_type x1, other arithmetic, per_device(): return result.astype(jnp.bfloat16)  6.5 us
  transfers between devices with their start and end apart: 1, of which 1 were waited for; matrix products, arithmetic and copies ran while one was open for 1% of the time, Pallas kernels for 0%

commit v1 on v0

--- a/solution.py
+++ b/solution.py
@@ -6,6 +6,11 @@
 W_DEV = 32
 NSAMP = 256
 EPS = 1e-06
+
+
+def gather_over(shard, axis, d):
+    sent = jnp.stack([shard] * lax.axis_size(axis))
+    return jnp.concatenate(lax.all_to_all(sent, axis, 0, 0), axis=d)
 
 
 def stack_blocks(blocks, scale, mate_index, first, count):
@@ -36,7 +41,7 @@
     groups = lax.axis_size("win")
     chosen = nblocks // groups
     first = lax.axis_index("win") * chosen
-    gathered = lax.all_gather(mixed, "win", axis=2, tiled=True)
+    gathered = gather_over(mixed, "win", 2)
     tallies = lax.all_gather(counts, "win", axis=0, tiled=True)
     weight = weights_of(tallies, partner)
     norm = jnp.sqrt(jnp.sum(weight * weight, axis=2))

time: 241 us -> 244 us (1.012)
  blocking collectives: 72.6 us -> 157 us
  waiting for transfers between devices: 72.9 us -> 0.01 us
  between operations: 13.5 us -> 0.11 us
  starting transfers between devices: 0.01 us -> 9.53 us
  local copies, waits for them, and re-layouts: 36.3 us -> 32.9 us
    all_gather x1, blocking collectives: 9.03 us -> 93.8 us  [per_device(): tallies = lax.all_gather(counts, 'win', axis=0, tiled=True)]
    all_gather x1 -> x0, waiting for transfers between devices: 72.9 us -> none  [per_device(): gathered = lax.all_gather(mixed, 'win', axis=2, tiled=True)]
    all_to_all x0 -> x1, starting transfers between devices: none -> 9.53 us  [gather_over(): return jnp.concatenate(lax.all_to_all(sent, axis, 0, 0), axis=d)]
    reshape x1 -> x0, local copies, waits for them, and re-layouts: 9.15 us -> none  [per_device(): blocks = gathered.reshape(nblocks, local_bins, groups, W_DEV, 2, width)]
    another operation x0 -> x2, local copies, waits for them, and re-layouts: none -> 6.23 us  [gather_over(): sent = jnp.stack([shard] * lax.axis_size(axis))]
    gather x1 -> x2, local copies, waits for them, and re-layouts: 6.48 us -> 9.67 us  [stack_blocks(): mates = jnp.take(blocks, mate_index, axis=0)]
  transfers between devices with their start and end apart: 1 -> 1, of which waited for: 1 -> 0; matrix products, arithmetic and copies ran while one was open for 1% -> 1% of each run, Pallas kernels for 0% -> 0%
where the time goes in v1:
time: 244 us; the launch traced here: 243 us
  blocking collectives  157 us (64%)
  local copies, waits for them, and re-layouts  32.9 us (13%)
  other arithmetic  31.2 us (13%)
  matrix products  11.9 us (5%)
  starting transfers between devices  9.53 us (4%)
    all_gather x1, blocking collectives, per_device(): tallies = lax.all_gather(counts, 'win', axis=0, tiled=True)  93.8 us
    all_to_all x1, blocking collectives, per_device(): lax.all_to_all(whitened, 'chan', split_axis=1, concat_axis=0, tiled=True)  63.5 us
    reduce_sum x1, other arithmetic, per_device(): total = jnp.sum(partial_value.astype(jnp.float32), axis=3)  13 us
    dot_general x1, matrix products, stack_blocks(): jnp.einsum('nrfgwkc,nrfgwkod->nrfgcod', weighted, paired, preferred_eleme...  11.9 us
    gather x2, local copies, waits for them, and re-layouts, stack_blocks(): mates = jnp.take(blocks, mate_index, axis=0)  9.67 us
    all_to_all x1, starting transfers between devices, gather_over(): return jnp.concatenate(lax.all_to_all(sent, axis, 0, 0), axis=d)  9.53 us
    reduce_sum x1, local copies, waits for them, and re-layouts, per_device(): total = jnp.sum(partial_value.astype(jnp.float32), axis=3)  9.27 us
    convert_element_type x1, other arithmetic, per_device(): return result.astype(jnp.bfloat16)  6.5 us
  transfers between devices with their start and end apart: 1, of which 0 were waited for; matrix products, arithmetic and copies ran while one was open for 1% of the time, Pallas kernels for 0%

profile of v1, /device:TPU:1, one launch (start us, length us, event | category | flops | bytes accessed | tf_op | source)
XLA Modules:
  0.0 242.9 jit_solution(15499896368749880166)
XLA Ops:
  0.0 3.8 %fusion.4 = f32[32,128]{1,0:T(8,128)S(1)} fusion(bf16[1,128,32,2,128]{4,3,2,1,0:T(2,128)(2,1)} %param.3), kind=kLoop, calls=%fused_computation.12 | loop fusion | flops 3141632 | bytes 2113536 | tf_op jit(solution)/shard_map/reduce_sum | solution.py:34
  3.8 3.8 %fusion.5 = bf16[1,128,32,2,128]{4,3,2,0,1:T(2,128)(2,1)S(1)} fusion(bf16[1,128,32,2,128]{4,3,2,1,0:T(2,128)(2,1)} %param.3, f32[32,128]{1,0:T(8,128)S(1)} %add_rsqrt_fusion), kind=kLoop, calls=%fused_computation.13 | loop fusion | flops 3145728 | bytes 4210688 | tf_op jit(solution)/shard_map/convert_element_type | solution.py:35
  7.6 63.5 %all_to_all.14 = bf16[1,128,32,2,128]{4,3,2,0,1:T(2,128)(2,1)S(1)} all-to-all(bf16[1,128,32,2,128]{4,3,2,0,1:T(2,128)(2,1)S(1)} %fusion.5), channel_id=1, replica_groups=mesh['chan'=64,'win'=4] {'chan'}, dimensions={1} | all-to-all | bytes 4194304 | tf_op jit(solution)/shard_map/all_to_all | solution.py:36
  71.2 0.6 copy.30
  71.8 5.6 %stack.21 = bf16[4,64,2,32,2,128]{5,3,4,2,1,0:T(8,128)(2,1)} broadcast(bf16[64,2,32,2,128]{4,2,3,1,0:T(8,128)(2,1)S(1)} %copy.30), dimensions={1,2,3,4,5} | broadcast | bytes 10485760 | tf_op jit(solution)/shard_map/stack | solution.py:12
  77.4 0.0 copy-start.1
  77.4 0.0 copy-start
  77.4 9.5 %all-to-all-start.1 = ((bf16[4,64,2,32,2,128]{5,3,4,2,1,0:T(8,128)(2,1)}), bf16[4,64,2,32,2,128]{5,3,4,2,1,0:T(8,128)(2,1)}, u32[]{:S(2)}, u32[]{:S(2)}) async-start(bf16[4,64,2,32,2,128]{5,3,4,2,1,0:T(8,128)(2,1)} %stack.21), calls=%async_computation.1 | async-start | bytes 16777216 | tf_op jit(solution)/shard_map/all_to_all | solution.py:13
  86.9 0.0 copy-done.1
  86.9 0.1 compare_and_fusion
  87.0 0.1 copy.33
  87.1 0.1 reshape.58
  87.2 0.1 copy.32
  87.3 0.0 copy-done
  87.3 93.8 %all_gather.3 = s32[128,64]{1,0:T(8,128)S(1)} all-gather(s32[32,64]{1,0:T(8,128)S(1)} %copy-done), channel_id=1, replica_groups=mesh['chan'=64,'win'=4] {'win'}, dimensions={0}, use_global_device_ids=true | all-gather | bytes 40960 | tf_op jit(solution)/shard_map/all_gather | solution.py:45
  181.1 0.1 copy.27
  181.2 0.1 reshape.50
  181.3 0.6 gather_fusion
  181.9 0.2 multiply_reduce_fusion
  182.1 0.1 mul.33
  182.2 0.1 dynamic-slice_bitcast_fusion.1
  182.3 0.1 copy.38
  182.4 0.0 all-to-all-done.1
  182.4 6.5 %gather_fusion.1 = bf16[32,2,4,32,2,128]{5,3,4,1,2,0:T(8,128)(2,1)} fusion(bf16[64,2,4,32,2,128]{5,3,4,1,0,2:T(8,128)(2,1)} %bitcast.9, s32[1024]{0:T(1024)S(1)} %pad_clamp_fusion), kind=kCustom, calls=%fused_computation.1 | custom fusion | bytes 8388736 | tf_op jit(solution)/shard_map/jit(_take)/gather | solution.py:18
  188.9 3.2 %copy.34 = bf16[32,2,4,32,2,128]{5,3,4,2,1,0:T(8,128)(2,1)S(1)} copy(bf16[32,2,4,32,2,128]{5,3,4,1,2,0:T(8,128)(2,1)} %gather_fusion.1) | data formatting | bytes 8388608 | tf_op jit(solution)/shard_map/jit(_take)/gather | solution.py:18
  192.1 0.5 broadcast_select_fusion
  192.6 0.4 slice_negate_fusion
  193.0 0.5 broadcast_select_fusion.1
  193.4 2.4 maximum_bitcast_fusion
  195.8 11.9 %bitcast_convert_fusion = bf16[16,2,2,4,128,2,128]{6,4,5,3,2,1,0:T(8,128)(2,1)} fusion(bf16[16,2,2,4,32,2,1,128]{7,4,5,6,3,2,1,0:T(8,128)(2,1)} %maximum_bitcast_fusion, bf16[16,2,2,4,32,2,1,128]{7,4,5,6,3,2,1,0:T(8,128)(2,1)S(1)} %broadcast_select_fusion.1, f32[16,2,4,32]{3,2,0,1:T(4,128)S(1)} %mul.33, bf16[4,64,2,32,2,128]{5,3,4,2,1,0:T(8,128)(2,1)} %all-to-all-done.1, ...), kind=kOutput, calls=%fused_computation.2 | convolution fusion | flops 1104150528 | bytes 27279364 | tf_op jit(solution)/shard_map/nrfgwkc,nrfgwkod->nrfgcod/dot_general | solution.py:22
  207.7 13.0 %convert_reduce_fusion = f32[16,2,2,128,2,128]{5,3,4,2,1,0:T(8,128)} fusion(bf16[16,2,2,4,128,2,128]{6,4,5,3,2,1,0:T(8,128)(2,1)} %bitcast_convert_fusion), kind=kLoop, calls=%fused_computation.3 | loop fusion | flops 14680064 | bytes 25165824 | tf_op jit(solution)/shard_map/reduce_sum | solution.py:54
  220.7 9.3 %copy.37 = f32[16,2,2,128,2,128]{3,5,4,2,1,0:T(8,128)} copy(f32[16,2,2,128,2,128]{5,3,4,2,1,0:T(8,128)} %convert_reduce_fusion) | data formatting | bytes 16777216 | tf_op jit(solution)/shard_map/reduce_sum | solution.py:54
  230.0 6.5 %fusion.3 = bf16[16,2,2,128,256]{3,4,2,1,0:T(8,128)(2,1)} fusion(f32[16,2,2,128,2,128]{3,5,4,2,1,0:T(8,128)} %copy.37, f32[16,2]{1,0:T(8,128)S(1)} %copy.38), kind=kLoop, calls=%fused_computation.8 | loop fusion | flops 4194304 | bytes 12583040 | tf_op jit(solution)/shard_map/convert_element_type | solution.py:58
  236.5 6.4 %copy.39 = bf16[16,2,2,128,256]{4,3,2,1,0:T(8,128)(2,1)} copy(bf16[16,2,2,128,256]{3,4,2,1,0:T(8,128)(2,1)} %fusion.3) | data formatting | bytes 8388608 | tf_op jit(solution)/shard_map/convert_element_type | solution.py:58
  (8 shorter events, 0.1 us)
Async XLA Ops:
  77.4 9.5 %copy-start.1 = (s32[2,64]{1,0:T(2,128)S(1)}, s32[2,64]{1,0:T(2,128)}, u32[]{:S(2)}) copy-start(s32[2,64]{1,0:T(2,128)} %param.5) | copy-start | bytes 1540
  77.4 9.9 %copy-start = (s32[32,64]{1,0:T(8,128)S(1)}, s32[32,64]{1,0:T(8,128)}, u32[]{:S(2)}) copy-start(s32[32,64]{1,0:T(8,128)} %param.4) | copy-start | bytes 24580
  77.4 105.0 %all-to-all-start.1 = ((bf16[4,64,2,32,2,128]{5,3,4,2,1,0:T(8,128)(2,1)}), bf16[4,64,2,32,2,128]{5,3,4,2,1,0:T(8,128)(2,1)}, u32[]{:S(2)}, u32[]{:S(2)}) async-start(bf16[4,64,2,32,2,128]{5,3,4,2,1,0:T(8,128)(2,1)} %stack.21), calls=%async_computation.1 | async-start | bytes 16777216 | tf_op jit(solution)/shard_map/all_to_all | solution.py:13
